TPU v7x, 128 devices: a whole 4x4x4 slice. The times are simulated.
128 devices in a mesh: var: 64 (over z, y, x), samp: 2 (over core).
Axes of the slice: x: 4, y: 4, z: 4, core: 2. Of those that a mesh axis runs over, the one named last changes fastest.
Arguments:
- dosages: bfloat16 [8192, 32768], P(('var', 'samp'))
- band_width: int32 [256], P('var'), may hold values from 7 to 8, as said below
Outputs:
- ld_tiles: float32 [256, 9, 128, 128], P('var', None, 'samp')
Inputs may be any that keep to these rules, and one draw needn't show every extreme that they name: `band_width`: some panel has band width 8, and some other panel has band width 8 - 1.
All inputs are finite; a program needn't handle non-finite values.
Results may differ from a plain program's by a relative error of at most 0.00092.
Values may be sent and summed in bfloat16 or wider, within the bound.
A program may use at most 128 MiB of HBM per device.

v0:
```python
import jax
import jax.numpy as jnp
from jax import lax
from jax.experimental import pallas as pl
from jax.experimental.pallas import tpu as pltpu
from jax.sharding import PartitionSpec as P

MESH = pl.DeviceIdType.MESH
WMAX = 8
PANEL = 128
SIDE = 4
GROUPS = SIDE * SIDE
OWN = 4
CHUNK = OWN * PANEL
REACH = WMAX // OWN
CHUNKS = SIDE + REACH
ROWS = 64
LOCAL = GROUPS * ROWS
BLOCK = 2 * PANEL
STEPS = [(chunk, 0, CHUNK) for chunk in range(CHUNKS - 1)] + [(CHUNKS - 1, first, BLOCK) for first in (0, BLOCK)]
AHEAD = 8
ORDER = [10, 15, 1, 4, 6, 3, 9, 12, 11, 14, 7, 13, 2, 8, 5]
SAMPLES = 8192
PLACES = [
    [(p, q) for q in range(OWN) for p in range(OWN) if 0 <= d * OWN + q - p <= WMAX] for d in range(REACH + 1)
]
STARTS = [sum(len(places) for places in PLACES[:d]) for d in range(REACH + 2)]
TILES = STARTS[-1]


def position():
    var = lax.axis_index("var")
    return var // SIDE, lax.rem(var, SIDE), lax.axis_index("samp")


def tiles_kernel(
    dos_ref, out_ref, staged, received, moments, gathered, sums, totals, standard, turned, part, twin, relay, ring,
    stage_sem, own_sem, swap_send, swap_recv, group_send, group_recv, stat_send, stat_recv, twin_send, twin_recv, relay_recv, ring_send, ring_recv,
):
    group, x, core = position()
    z, y = group // SIDE, lax.rem(group, SIDE)

    def stage(index):
        first = pl.multiple_of(index * CHUNK, CHUNK)
        return pltpu.make_async_copy(dos_ref.at[:, pl.ds(first, CHUNK)], staged.at[index], stage_sem.at[index])

    def stage_begin(index, carry):
        stage(index).start()
        return carry

    def stage_end(index, carry):
        stage(index).wait()
        return carry

    lax.fori_loop(0, GROUPS * SIDE, stage_begin, 0)

    peers = []
    for dx in range(SIDE):
        for dc in range(2):
            if dx or dc:
                peer_x, peer_c = lax.rem(x + dx, SIDE), lax.rem(core + dc, 2)
                peers.append((group * SIDE + peer_x, peer_c))

    def group_at(offset):
        return lax.rem(z + offset // SIDE, SIDE) * SIDE + lax.rem(y + offset % SIDE, SIDE)

    barrier = pltpu.get_barrier_semaphore()
    for offset in range(1, GROUPS):
        pl.semaphore_signal(
            barrier, inc=1, device_id=(group_at(offset) * SIDE + x, core), device_id_type=MESH
        )
    for peer in peers:
        pl.semaphore_signal(barrier, inc=1, device_id=peer, device_id_type=MESH)
    lax.fori_loop(0, GROUPS * SIDE, stage_end, 0)
    pl.semaphore_wait(barrier, GROUPS - 1 + len(peers))

    def swap(index):
        step, turn = divmod(index, GROUPS - 1)
        chunk, first, count = STEPS[step]
        columns = pl.ds(first, count)
        offset = ORDER[turn]
        other = group_at(offset)
        return pltpu.make_async_remote_copy(
            src_ref=staged.at[lax.rem(other * SIDE + chunk, GROUPS * SIDE), :, columns],
            dst_ref=received.at[chunk, offset, :, columns],
            send_sem=swap_send.at[step, offset],
            recv_sem=swap_recv.at[step, offset],
            device_id=(other * SIDE + x, core),
            device_id_type=MESH,
        )

    swaps = [swap(index) for index in range(len(STEPS) * (GROUPS - 1))]
    started = [0]

    def pump(count):
        for index in range(started[0], min(started[0] + count, len(swaps))):
            if index >= AHEAD:
                swaps[index - AHEAD].wait_send()
            swaps[index].start()
            started[0] = index + 1

    def own_copy(step):
        chunk, first, count = STEPS[step]
        columns = pl.ds(first, count)
        return pltpu.make_async_copy(
            staged.at[lax.rem(group * SIDE + chunk, GROUPS * SIDE), :, columns],
            received.at[chunk, 0, :, columns],
            own_sem.at[step],
        )

    def swap_end(step):
        own_copy(step).wait()
        for copy in swaps[step * (GROUPS - 1):(step + 1) * (GROUPS - 1)]:
            copy.wait_recv()

    def local_moments():
        def chunk_moments(index, carry):
            values = staged[index].astype(jnp.float32).reshape(ROWS // 8, 8, CHUNK)
            for row, total in enumerate((jnp.sum(values, 0), jnp.sum(values * values, 0))):
                total = jnp.sum(total, 0, keepdims=True)
                for q in range(OWN):
                    moments[index, row * OWN + q:row * OWN + q + 1, :] = total[:, q * PANEL:(q + 1) * PANEL]
            return carry

        lax.fori_loop(0, GROUPS * SIDE, chunk_moments, 0)
        for extra in range(REACH):
            moments[GROUPS * SIDE + extra] = moments[extra]

    def group_moments_begin():
        gathered[0] = moments[pl.ds(group * SIDE, CHUNKS)]
        copies = []
        for offset in range(1, GROUPS):
            other = group_at(offset)
            copy = pltpu.make_async_remote_copy(
                src_ref=moments.at[pl.ds(other * SIDE, CHUNKS)],
                dst_ref=gathered.at[offset],
                send_sem=group_send.at[offset],
                recv_sem=group_recv.at[offset],
                device_id=(other * SIDE + x, core),
                device_id_type=MESH,
            )
            copy.start()
            copies.append(copy)
        return copies

    def ring_moments_begin(copies):
        for copy in copies:
            copy.wait()
        sums[0] = jnp.sum(gathered[...], 0)
        copies = []
        for index, peer in enumerate(peers):
            copy = pltpu.make_async_remote_copy(
                src_ref=sums.at[0],
                dst_ref=sums.at[index + 1],
                send_sem=stat_send.at[index],
                recv_sem=stat_recv.at[index],
                device_id=peer,
                device_id_type=MESH,
            )
            copy.start()
            copies.append(copy)
        return copies

    def ring_moments_end(copies):
        for copy in copies:
            copy.wait()
        totals[...] = jnp.sum(sums[...], 0)

    def standardize(step):
        chunk, start, count = STEPS[step]
        columns = pl.ds(start, count)
        panels = range(start // PANEL, (start + count) // PANEL)
        first, second = totals[chunk, 0:OWN], totals[chunk, OWN:2 * OWN]
        mean = first * (1.0 / SAMPLES)
        inv_scale = lax.rsqrt(second * (1.0 / SAMPLES) - mean * mean + 1e-05)
        mean = jnp.concatenate([mean[q:q + 1] for q in panels], axis=1)
        inv_scale = jnp.concatenate([inv_scale[q:q + 1] for q in panels], axis=1)

        def block_standard(block, carry):
            rows = pl.ds(pl.multiple_of(block * ROWS, ROWS), ROWS)
            values = received[chunk, block, :, columns].astype(jnp.float32)
            standard[chunk, rows, columns] = ((values - mean) * inv_scale).astype(jnp.bfloat16)
            return carry

        lax.fori_loop(0, GROUPS, block_standard, 0)
        if chunk < SIDE:
            turned[chunk] = standard[chunk].T

    def pieces_of(step):
        chunk, start, count = STEPS[step]
        pieces = []
        for d in range(REACH + 1):
            if 0 <= chunk - d < SIDE:
                inside = [
                    index for index, (p, q) in enumerate(PLACES[d])
                    if start // PANEL <= q < (start + count) // PANEL
                ]
                pieces.append((chunk - d, d, d + (start > 0), STARTS[d] + inside[0], len(inside)))
        return pieces

    def twin_copy(rows_chunk, number, first, count):
        which = pl.ds(first, count)
        return pltpu.make_async_remote_copy(
            src_ref=part.at[rows_chunk, 1 - core, which],
            dst_ref=twin.at[rows_chunk, which],
            send_sem=twin_send.at[rows_chunk, number],
            recv_sem=twin_recv.at[rows_chunk, number],
            device_id=(group * SIDE + x, 1 - core),
            device_id_type=MESH,
        )

    def multiply(step):
        chunk, start, columns = STEPS[step]
        for rows_chunk, d, number, first, count in pieces_of(step):
            for pp in range(OWN // 2):
                for qq in range(start // BLOCK, (start + columns) // BLOCK):
                    inside = [
                        (p, q) for p in range(2) for q in range(2) if (2 * pp + p, 2 * qq + q) in PLACES[d]
                    ]
                    if not inside:
                        continue
                    block = jnp.dot(
                        turned[rows_chunk, pp * BLOCK:(pp + 1) * BLOCK, :],
                        standard[chunk, :, qq * BLOCK:(qq + 1) * BLOCK],
                        preferred_element_type=jnp.float32,
                    )
                    for p, q in inside:
                        tile = STARTS[d] + PLACES[d].index((2 * pp + p, 2 * qq + q))
                        for half in range(2):
                            top = p * PANEL + half * (PANEL // 2)
                            part[rows_chunk, half, tile] = block[
                                top:top + PANEL // 2, q * PANEL:(q + 1) * PANEL
                            ]
            twin_copy(rows_chunk, number, first, count).start()

    def halves_of(first, count):
        upper = (count + 1) // 2
        return pl.ds(first, upper), pl.ds(first + upper, count - upper)

    def line_copy(rows_chunk, number, halves, half, way, relayed):
        which = halves[half]
        return pltpu.make_async_remote_copy(
            src_ref=part.at[rows_chunk, core, which],
            dst_ref=(relay if relayed else ring).at[way, which],
            send_sem=ring_send.at[rows_chunk, number, half],
            recv_sem=relay_recv.at[way, number] if relayed else ring_recv.at[way, number, half],
            device_id=(group * SIDE + lax.rem(x + 1 + 2 * way, SIDE), core),
            device_id_type=MESH,
        )

    def reduce(step):
        for rows_chunk, d, number, first, count in pieces_of(step):
            which = pl.ds(first, count)
            halves = halves_of(first, count)
            twin_copy(rows_chunk, number, first, count).wait()
            part[rows_chunk, core, which] = part[rows_chunk, core, which] + twin[rows_chunk, which]
            distance = lax.rem(rows_chunk - x + SIDE, SIDE)

            @pl.when(distance == 2)
            def _():
                line_copy(rows_chunk, number, halves, 0, 0, True).start()
                line_copy(rows_chunk, number, halves, 1, 1, True).start()

            @pl.when(distance == 1)
            def _():
                line_copy(rows_chunk, number, halves, 1, 0, False).start()

            @pl.when(distance == 3)
            def _():
                line_copy(rows_chunk, number, halves, 0, 1, False).start()

        pump(5)
        for rows_chunk, d, number, first, count in pieces_of(step):
            halves = halves_of(first, count)
            distance = lax.rem(rows_chunk - x + SIDE, SIDE)
            for way in range(2):

                @pl.when(distance == 1 + 2 * way)
                def _():
                    which = halves[way]
                    line_copy(rows_chunk, number, halves, way, way, True).wait_recv()
                    part[rows_chunk, core, which] = part[rows_chunk, core, which] + relay[way, which]
                    line_copy(rows_chunk, number, halves, way, way, False).start()

    pump(4)
    for step in range(len(STEPS)):
        own_copy(step).start()
    local_moments()
    copies = group_moments_begin()
    pump(8)
    copies = ring_moments_begin(copies)
    pump(8)
    ring_moments_end(copies)
    for step in range(len(STEPS)):
        pump((step + 1) * (GROUPS - 1) + AHEAD - started[0])
        swap_end(step)
        standardize(step)
        multiply(step)
        pump(3)
        reduce(step)
        pump(3)
    for copy in swaps[-AHEAD:]:
        copy.wait_send()

    for step in range(len(STEPS)):
        for rows_chunk, d, number, first, count in pieces_of(step):
            halves = halves_of(first, count)

            @pl.when(x != rows_chunk)
            def _():
                for half in range(2):
                    line_copy(rows_chunk, number, halves, half, 0, False).wait_send()

            @pl.when(x == rows_chunk)
            def _():
                for way in range(2):
                    for half in range(2):
                        line_copy(rows_chunk, number, halves, half, way, False).wait_recv()

    for d in range(REACH + 1):
        for index, (p, q) in enumerate(PLACES[d]):
            tile = STARTS[d] + index
            out_ref[p, d * OWN + q - p] = part[x, core, tile] + (ring[0, tile] + ring[1, tile])


def tiles(dosages):
    half_tile = (PANEL // 2, PANEL)
    dma = pltpu.SemaphoreType.DMA
    return pl.pallas_call(
        tiles_kernel,
        out_shape=jax.ShapeDtypeStruct((OWN, WMAX + 1) + half_tile, jnp.float32),
        in_specs=[pl.BlockSpec(memory_space=pl.ANY)],
        out_specs=pl.BlockSpec(memory_space=pltpu.VMEM),
        scratch_shapes=[
            pltpu.VMEM((GROUPS * SIDE, ROWS, CHUNK), jnp.bfloat16),
            pltpu.VMEM((CHUNKS, GROUPS, ROWS, CHUNK), jnp.bfloat16),
            pltpu.VMEM((GROUPS * SIDE + REACH, 2 * OWN, PANEL), jnp.float32),
            pltpu.VMEM((GROUPS, CHUNKS, 2 * OWN, PANEL), jnp.float32),
            pltpu.VMEM((8, CHUNKS, 2 * OWN, PANEL), jnp.float32),
            pltpu.VMEM((CHUNKS, 2 * OWN, PANEL), jnp.float32),
            pltpu.VMEM((CHUNKS, LOCAL, CHUNK), jnp.bfloat16),
            pltpu.VMEM((SIDE, CHUNK, LOCAL), jnp.bfloat16),
            pltpu.VMEM((SIDE, 2, TILES) + half_tile, jnp.float32),
            pltpu.VMEM((SIDE, TILES) + half_tile, jnp.float32),
            pltpu.VMEM((2, TILES) + half_tile, jnp.float32),
            pltpu.VMEM((2, TILES) + half_tile, jnp.float32),
            dma((GROUPS * SIDE,)),
            dma((len(STEPS),)),
            dma((len(STEPS), GROUPS)),
            dma((len(STEPS), GROUPS)),
            dma((GROUPS,)),
            dma((GROUPS,)),
            dma((7,)),
            dma((7,)),
            dma((SIDE, REACH + 2)),
            dma((SIDE, REACH + 2)),
            dma((2, REACH + 2)),
            dma((SIDE, REACH + 2, 2)),
            dma((2, REACH + 2, 2)),
        ],
        compiler_params=pltpu.CompilerParams(
            collective_id=0, has_side_effects=True, vmem_limit_bytes=60 * 1024 * 1024
        ),
        name="tiles",
    )(dosages)


def per_device(dosages, band_width):
    band_tiles = tiles(dosages)
    offsets = jnp.arange(WMAX + 1, dtype=jnp.int32)
    panel_count = OWN * lax.axis_size("var")
    global_panel = lax.axis_index("var") * OWN + jnp.arange(OWN, dtype=jnp.int32)
    in_band = (offsets[None, :] <= band_width[:, None]) & (
        global_panel[:, None] + offsets[None, :] < panel_count
    )
    return jnp.where(in_band[:, :, None, None], band_tiles * (1.0 / SAMPLES), 0.0)


def solution(mesh):
    in_specs = (P(("var", "samp"), None), P("var"))
    out_specs = P("var", None, "samp", None)
    return jax.shard_map(
        per_device, mesh=mesh, in_specs=in_specs, out_specs=out_specs, check_vma=False
    )
```

profile of v0, /device:TPU:7, one launch (start us, length us, event | category | flops | bytes accessed | tf_op | source)
XLA Modules:
  0.0 117.2 jit_solution(16174751757250787992)
XLA Ops:
  0.0 0.7 fusion
  0.7 114.0 %tiles.1 = f32[4,9,64,128]{3,2,1,0:T(8,128)} custom-call(bf16[64,32768]{1,0:T(8,128)(2,1)} %dos_ref.1), custom_call_target="tpu_custom_call" | custom-call | tf_op jit(solution)/shard_map/tiles/pallas_call | solution.py:329
  114.7 2.5 %multiply_select_fusion = f32[4,9,64,128]{3,2,1,0:T(8,128)} fusion(f32[4,9,64,128]{3,2,1,0:T(8,128)} %tiles.1, pred[4,9]{1,0:T(4,128)(4,1)S(1)} %fusion), kind=kLoop, calls=%fused_computation | loop fusion | flops 589824 | bytes 2359332 | tf_op jit(solution)/shard_map/jit(_where)/select_n | solution.py:376
  (1 shorter events, 0.0 us)
where the time goes:
time: 117 us
  Pallas kernels  114 us (97%)
  other arithmetic  3.18 us (3%)
    pallas_call x1, Pallas kernels, tiles(): pl.pallas_call(tiles_kernel, out_shape=jax.ShapeDtypeStruct((OWN, WMAX +...  114 us
    select_n x1, other arithmetic, per_device(): jnp.where(in_band[:, :, None, None], band_tiles * (1.0 / SAMPLES), 0.0)  2.45 us

commit v1 on v0

--- a/solution.py
+++ b/solution.py
@@ -18,7 +18,7 @@
 LOCAL = GROUPS * ROWS
 BLOCK = 2 * PANEL
 STEPS = [(chunk, 0, CHUNK) for chunk in range(CHUNKS - 1)] + [(CHUNKS - 1, first, BLOCK) for first in (0, BLOCK)]
-AHEAD = 8
+AHEAD = 15
 ORDER = [10, 15, 1, 4, 6, 3, 9, 12, 11, 14, 7, 13, 2, 8, 5]
 SAMPLES = 8192
 PLACES = [
@@ -282,7 +282,7 @@
                     part[rows_chunk, core, which] = part[rows_chunk, core, which] + relay[way, which]
                     line_copy(rows_chunk, number, halves, way, way, False).start()
 
-    pump(4)
+    pump(8)
     for step in range(len(STEPS)):
         own_copy(step).start()
     local_moments()

time: 117 us -> 116 us (level)
  Pallas kernels: 114 us -> 112 us
    pallas_call x1, Pallas kernels: 114 us -> 112 us  [tiles(): pl.pallas_call(tiles_kernel, out_shape=jax.ShapeDtypeStruct((OWN, WMAX +...]
where the time goes in v1:
time: 116 us; the launch traced here: 115 us
  Pallas kernels  112 us (97%)
  other arithmetic  3.18 us (3%)
    pallas_call x1, Pallas kernels, tiles(): pl.pallas_call(tiles_kernel, out_shape=jax.ShapeDtypeStruct((OWN, WMAX +...  112 us
    select_n x1, other arithmetic, per_device(): jnp.where(in_band[:, :, None, None], band_tiles * (1.0 / SAMPLES), 0.0)  2.45 us

profile of v1, /device:TPU:7, one launch (start us, length us, event | category | flops | bytes accessed | tf_op | source)
XLA Modules:
  0.0 115.3 jit_solution(5238158450038295192)
XLA Ops:
  0.0 0.7 fusion
  0.7 112.1 %tiles.1 = f32[4,9,64,128]{3,2,1,0:T(8,128)} custom-call(bf16[64,32768]{1,0:T(8,128)(2,1)} %dos_ref.1), custom_call_target="tpu_custom_call" | custom-call | tf_op jit(solution)/shard_map/tiles/pallas_call | solution.py:329
  112.8 2.5 %multiply_select_fusion = f32[4,9,64,128]{3,2,1,0:T(8,128)} fusion(f32[4,9,64,128]{3,2,1,0:T(8,128)} %tiles.1, pred[4,9]{1,0:T(4,128)(4,1)S(1)} %fusion), kind=kLoop, calls=%fused_computation | loop fusion | flops 589824 | bytes 2359332 | tf_op jit(solution)/shard_map/jit(_where)/select_n | solution.py:376
  (1 shorter events, 0.0 us)

commit v2 on v1

--- a/solution.py
+++ b/solution.py
@@ -71,8 +71,11 @@
         )
     for peer in peers:
         pl.semaphore_signal(barrier, inc=1, device_id=peer, device_id_type=MESH)
-    lax.fori_loop(0, GROUPS * SIDE, stage_end, 0)
     pl.semaphore_wait(barrier, GROUPS - 1 + len(peers))
+
+    def columns_of(other, chunk, first, count):
+        top = lax.rem(other * SIDE + chunk, GROUPS * SIDE) * CHUNK + first
+        return dos_ref.at[:, pl.ds(pl.multiple_of(top, BLOCK), count)]
 
     def swap(index):
         step, turn = divmod(index, GROUPS - 1)
@@ -81,7 +84,7 @@
         offset = ORDER[turn]
         other = group_at(offset)
         return pltpu.make_async_remote_copy(
-            src_ref=staged.at[lax.rem(other * SIDE + chunk, GROUPS * SIDE), :, columns],
+            src_ref=columns_of(other, chunk, first, count),
             dst_ref=received.at[chunk, offset, :, columns],
             send_sem=swap_send.at[step, offset],
             recv_sem=swap_recv.at[step, offset],
@@ -103,7 +106,7 @@
         chunk, first, count = STEPS[step]
         columns = pl.ds(first, count)
         return pltpu.make_async_copy(
-            staged.at[lax.rem(group * SIDE + chunk, GROUPS * SIDE), :, columns],
+            columns_of(group, chunk, first, count),
             received.at[chunk, 0, :, columns],
             own_sem.at[step],
         )
@@ -269,7 +272,9 @@
             def _():
                 line_copy(rows_chunk, number, halves, 0, 1, False).start()
 
-        pump(5)
+            pump(4)
+
+        pump(3)
         for rows_chunk, d, number, first, count in pieces_of(step):
             halves = halves_of(first, count)
             distance = lax.rem(rows_chunk - x + SIDE, SIDE)
@@ -285,6 +290,7 @@
     pump(8)
     for step in range(len(STEPS)):
         own_copy(step).start()
+    lax.fori_loop(0, GROUPS * SIDE, stage_end, 0)
     local_moments()
     copies = group_moments_begin()
     pump(8)
@@ -296,9 +302,8 @@
         swap_end(step)
         standardize(step)
         multiply(step)
-        pump(3)
+        pump(2)
         reduce(step)
-        pump(3)
     for copy in swaps[-AHEAD:]:
         copy.wait_send()
 

time: 116 us -> 115 us (level)
  no operation moved by 1% of the time
where the time goes in v2:
time: 115 us
  Pallas kernels  112 us (97%)
  other arithmetic  3.18 us (3%)
    pallas_call x1, Pallas kernels, tiles(): pl.pallas_call(tiles_kernel, out_shape=jax.ShapeDtypeStruct((OWN, WMAX +...  112 us
    select_n x1, other arithmetic, per_device(): jnp.where(in_band[:, :, None, None], band_tiles * (1.0 / SAMPLES), 0.0)  2.45 us

profile of v2, /device:TPU:7, one launch (start us, length us, event | category | flops | bytes accessed | tf_op | source)
XLA Modules:
  0.0 114.7 jit_solution(16846112867985717485)
XLA Ops:
  0.0 0.7 fusion
  0.7 111.5 %tiles.1 = f32[4,9,64,128]{3,2,1,0:T(8,128)} custom-call(bf16[64,32768]{1,0:T(8,128)(2,1)} %dos_ref.1), custom_call_target="tpu_custom_call" | custom-call | tf_op jit(solution)/shard_map/tiles/pallas_call | solution.py:334
  112.3 2.5 %multiply_select_fusion = f32[4,9,64,128]{3,2,1,0:T(8,128)} fusion(f32[4,9,64,128]{3,2,1,0:T(8,128)} %tiles.1, pred[4,9]{1,0:T(4,128)(4,1)S(1)} %fusion), kind=kLoop, calls=%fused_computation | loop fusion | flops 589824 | bytes 2359332 | tf_op jit(solution)/shard_map/jit(_where)/select_n | solution.py:381
  (1 shorter events, 0.0 us)

commit v3 on v2

--- a/solution.py
+++ b/solution.py
@@ -18,7 +18,7 @@
 LOCAL = GROUPS * ROWS
 BLOCK = 2 * PANEL
 STEPS = [(chunk, 0, CHUNK) for chunk in range(CHUNKS - 1)] + [(CHUNKS - 1, first, BLOCK) for first in (0, BLOCK)]
-AHEAD = 15
+AHEAD = 24
 ORDER = [10, 15, 1, 4, 6, 3, 9, 12, 11, 14, 7, 13, 2, 8, 5]
 SAMPLES = 8192
 PLACES = [
@@ -334,7 +334,7 @@
     return pl.pallas_call(
         tiles_kernel,
         out_shape=jax.ShapeDtypeStruct((OWN, WMAX + 1) + half_tile, jnp.float32),
-        in_specs=[pl.BlockSpec(memory_space=pl.ANY)],
+        in_specs=[pl.BlockSpec(memory_space=pltpu.HBM)],
         out_specs=pl.BlockSpec(memory_space=pltpu.VMEM),
         scratch_shapes=[
             pltpu.VMEM((GROUPS * SIDE, ROWS, CHUNK), jnp.bfloat16),
@@ -364,7 +364,7 @@
             dma((2, REACH + 2, 2)),
         ],
         compiler_params=pltpu.CompilerParams(
-            collective_id=0, has_side_effects=True, vmem_limit_bytes=60 * 1024 * 1024
+            collective_id=0, has_side_effects=True, vmem_limit_bytes=52 * 1024 * 1024
         ),
         name="tiles",
     )(dosages)

time: 115 us -> 113 us (0.983)
  other arithmetic: 3.18 us -> 1.91 us
    select_n x1, other arithmetic: 2.45 us -> 1.18 us  [per_device(): jnp.where(in_band[:, :, None, None], band_tiles * (1.0 / SAMPLES), 0.0)]
where the time goes in v3:
time: 113 us
  Pallas kernels  111 us (98%)
  other arithmetic  1.91 us (2%)
    pallas_call x1, Pallas kernels, tiles(): pl.pallas_call(tiles_kernel, out_shape=jax.ShapeDtypeStruct((OWN, WMAX +...  111 us

profile of v3, /device:TPU:7, one launch (start us, length us, event | category | flops | bytes accessed | tf_op | source)
XLA Modules:
  0.0 112.5 jit_solution(2757514611994983871)
XLA Ops:
  0.0 0.7 fusion
  0.7 110.6 %tiles.1 = f32[4,9,64,128]{3,2,1,0:T(8,128)S(1)} custom-call(bf16[64,32768]{1,0:T(8,128)(2,1)} %dos_ref.1), custom_call_target="tpu_custom_call" | custom-call | tf_op jit(solution)/shard_map/tiles/pallas_call | solution.py:334
  111.4 1.2 %multiply_select_fusion = f32[4,9,64,128]{3,2,1,0:T(8,128)} fusion(f32[4,9,64,128]{3,2,1,0:T(8,128)S(1)} %tiles.1, pred[4,9]{1,0:T(4,128)(4,1)S(1)} %fusion), kind=kLoop, calls=%fused_computation | loop fusion | flops 589824 | bytes 2359332 | tf_op jit(solution)/shard_map/jit(_where)/select_n | solution.py:381
  (1 shorter events, 0.0 us)

commit v4 on v3

--- a/solution.py
+++ b/solution.py
@@ -18,7 +18,8 @@
 LOCAL = GROUPS * ROWS
 BLOCK = 2 * PANEL
 STEPS = [(chunk, 0, CHUNK) for chunk in range(CHUNKS - 1)] + [(CHUNKS - 1, first, BLOCK) for first in (0, BLOCK)]
-AHEAD = 24
+AHEAD = 12
+PROMPT = len(STEPS) - 3
 ORDER = [10, 15, 1, 4, 6, 3, 9, 12, 11, 14, 7, 13, 2, 8, 5]
 SAMPLES = 8192
 PLACES = [
@@ -272,9 +273,7 @@
             def _():
                 line_copy(rows_chunk, number, halves, 0, 1, False).start()
 
-            pump(4)
-
-        pump(3)
+    def relay_on(step):
         for rows_chunk, d, number, first, count in pieces_of(step):
             halves = halves_of(first, count)
             distance = lax.rem(rows_chunk - x + SIDE, SIDE)
@@ -302,8 +301,12 @@
         swap_end(step)
         standardize(step)
         multiply(step)
-        pump(2)
+        if 1 <= step <= PROMPT:
+            relay_on(step - 1)
+        pump(AHEAD)
         reduce(step)
+        if step >= PROMPT:
+            relay_on(step)
     for copy in swaps[-AHEAD:]:
         copy.wait_send()
 

time: 113 us -> 115 us (1.018)
  no operation moved by 1% of the time
where the time goes in v4:
time: 115 us; the launch traced here: 114 us
  Pallas kernels  112 us (97%)
  other arithmetic  1.91 us (2%)
    pallas_call x1, Pallas kernels, tiles(): pl.pallas_call(tiles_kernel, out_shape=jax.ShapeDtypeStruct((OWN, WMAX +...  112 us

profile of v4, /device:TPU:7, one launch (start us, length us, event | category | flops | bytes accessed | tf_op | source)
XLA Modules:
  0.0 113.6 jit_solution(5767033464891723135)
XLA Ops:
  0.0 0.7 fusion
  0.7 111.7 %tiles.1 = f32[4,9,64,128]{3,2,1,0:T(8,128)S(1)} custom-call(bf16[64,32768]{1,0:T(8,128)(2,1)} %dos_ref.1), custom_call_target="tpu_custom_call" | custom-call | tf_op jit(solution)/shard_map/tiles/pallas_call | solution.py:337
  112.4 1.2 %multiply_select_fusion = f32[4,9,64,128]{3,2,1,0:T(8,128)} fusion(f32[4,9,64,128]{3,2,1,0:T(8,128)S(1)} %tiles.1, pred[4,9]{1,0:T(4,128)(4,1)S(1)} %fusion), kind=kLoop, calls=%fused_computation | loop fusion | flops 589824 | bytes 2359332 | tf_op jit(solution)/shard_map/jit(_where)/select_n | solution.py:384
  (1 shorter events, 0.0 us)

commit v5 on v3

--- a/solution.py
+++ b/solution.py
@@ -20,6 +20,7 @@
 STEPS = [(chunk, 0, CHUNK) for chunk in range(CHUNKS - 1)] + [(CHUNKS - 1, first, BLOCK) for first in (0, BLOCK)]
 AHEAD = 24
 ORDER = [10, 15, 1, 4, 6, 3, 9, 12, 11, 14, 7, 13, 2, 8, 5]
+PARTNER = [1, 0, 3, 2, 5, 4, 7, 6, 9, 8, 11, 10, 13, 12, 14]
 SAMPLES = 8192
 PLACES = [
     [(p, q) for q in range(OWN) for p in range(OWN) if 0 <= d * OWN + q - p <= WMAX] for d in range(REACH + 1)
@@ -62,7 +63,7 @@
                 peers.append((group * SIDE + peer_x, peer_c))
 
     def group_at(offset):
-        return lax.rem(z + offset // SIDE, SIDE) * SIDE + lax.rem(y + offset % SIDE, SIDE)
+        return lax.rem(z + offset // SIDE, SIDE) * SIDE + lax.rem(y + lax.rem(offset, SIDE), SIDE)
 
     barrier = pltpu.get_barrier_semaphore()
     for offset in range(1, GROUPS):
@@ -81,7 +82,7 @@
         step, turn = divmod(index, GROUPS - 1)
         chunk, first, count = STEPS[step]
         columns = pl.ds(first, count)
-        offset = ORDER[turn]
+        offset = ORDER[turn] + core * (ORDER[PARTNER[turn]] - ORDER[turn])
         other = group_at(offset)
         return pltpu.make_async_remote_copy(
             src_ref=columns_of(other, chunk, first, count),

time: 113 us -> 112 us (level)
  no operation moved by 1% of the time
where the time goes in v5:
time: 112 us
  Pallas kernels  110 us (98%)
  other arithmetic  1.91 us (2%)
    pallas_call x1, Pallas kernels, tiles(): pl.pallas_call(tiles_kernel, out_shape=jax.ShapeDtypeStruct((OWN, WMAX +...  110 us

profile of v5, /device:TPU:7, one launch (start us, length us, event | category | flops | bytes accessed | tf_op | source)
XLA Modules:
  0.0 112.4 jit_solution(15200448292384436256)
XLA Ops:
  0.0 0.7 fusion
  0.7 110.4 %tiles.1 = f32[4,9,64,128]{3,2,1,0:T(8,128)S(1)} custom-call(bf16[64,32768]{1,0:T(8,128)(2,1)} %dos_ref.1), custom_call_target="tpu_custom_call" | custom-call | tf_op jit(solution)/shard_map/tiles/pallas_call | solution.py:335
  111.2 1.2 %multiply_select_fusion = f32[4,9,64,128]{3,2,1,0:T(8,128)} fusion(f32[4,9,64,128]{3,2,1,0:T(8,128)S(1)} %tiles.1, pred[4,9]{1,0:T(4,128)(4,1)S(1)} %fusion), kind=kLoop, calls=%fused_computation | loop fusion | flops 589824 | bytes 2359332 | tf_op jit(solution)/shard_map/jit(_where)/select_n | solution.py:382
  (1 shorter events, 0.0 us)

commit v6 on v5

--- a/solution.py
+++ b/solution.py
@@ -17,7 +17,7 @@
 ROWS = 64
 LOCAL = GROUPS * ROWS
 BLOCK = 2 * PANEL
-STEPS = [(chunk, 0, CHUNK) for chunk in range(CHUNKS - 1)] + [(CHUNKS - 1, first, BLOCK) for first in (0, BLOCK)]
+STEPS = [(chunk, 0, CHUNK) for chunk in range(CHUNKS)]
 AHEAD = 24
 ORDER = [10, 15, 1, 4, 6, 3, 9, 12, 11, 14, 7, 13, 2, 8, 5]
 PARTNER = [1, 0, 3, 2, 5, 4, 7, 6, 9, 8, 11, 10, 13, 12, 14]

time: 112 us -> 111 us (level)
  Pallas kernels: 110 us -> 108 us
    pallas_call x1, Pallas kernels: 110 us -> 108 us  [tiles(): pl.pallas_call(tiles_kernel, out_shape=jax.ShapeDtypeStruct((OWN, WMAX +...]
where the time goes in v6:
time: 111 us; the launch traced here: 110 us
  Pallas kernels  108 us (97%)
  other arithmetic  1.91 us (2%)
    pallas_call x1, Pallas kernels, tiles(): pl.pallas_call(tiles_kernel, out_shape=jax.ShapeDtypeStruct((OWN, WMAX +...  108 us

profile of v6, /device:TPU:7, one launch (start us, length us, event | category | flops | bytes accessed | tf_op | source)
XLA Modules:
  0.0 110.4 jit_solution(6002577076110758316)
XLA Ops:
  0.0 0.7 fusion
  0.7 108.5 %tiles.1 = f32[4,9,64,128]{3,2,1,0:T(8,128)S(1)} custom-call(bf16[64,32768]{1,0:T(8,128)(2,1)} %dos_ref.1), custom_call_target="tpu_custom_call" | custom-call | tf_op jit(solution)/shard_map/tiles/pallas_call | solution.py:335
  109.2 1.2 %multiply_select_fusion = f32[4,9,64,128]{3,2,1,0:T(8,128)} fusion(f32[4,9,64,128]{3,2,1,0:T(8,128)S(1)} %tiles.1, pred[4,9]{1,0:T(4,128)(4,1)S(1)} %fusion), kind=kLoop, calls=%fused_computation | loop fusion | flops 589824 | bytes 2359332 | tf_op jit(solution)/shard_map/jit(_where)/select_n | solution.py:382
  (1 shorter events, 0.0 us)

commit v7 on v6

--- a/solution.py
+++ b/solution.py
@@ -273,9 +273,9 @@
             def _():
                 line_copy(rows_chunk, number, halves, 0, 1, False).start()
 
-            pump(4)
-
-        pump(3)
+            pump(2)
+
+        pump(2)
         for rows_chunk, d, number, first, count in pieces_of(step):
             halves = halves_of(first, count)
             distance = lax.rem(rows_chunk - x + SIDE, SIDE)
@@ -299,11 +299,11 @@
     pump(8)
     ring_moments_end(copies)
     for step in range(len(STEPS)):
-        pump((step + 1) * (GROUPS - 1) + AHEAD - started[0])
+        pump((step + 1) * (GROUPS - 1) + 8 - started[0])
         swap_end(step)
         standardize(step)
         multiply(step)
-        pump(2)
+        pump(7)
         reduce(step)
     for copy in swaps[-AHEAD:]:
         copy.wait_send()

time: 111 us -> 114 us (1.027); the launches traced: 110 us -> 112 us
  Pallas kernels: 108 us -> 110 us
    pallas_call x1, Pallas kernels: 108 us -> 110 us  [tiles(): pl.pallas_call(tiles_kernel, out_shape=jax.ShapeDtypeStruct((OWN, WMAX +...]
where the time goes in v7:
time: 114 us; the launch traced here: 112 us
  Pallas kernels  110 us (96%)
  other arithmetic  1.91 us (2%)
    pallas_call x1, Pallas kernels, tiles(): pl.pallas_call(tiles_kernel, out_shape=jax.ShapeDtypeStruct((OWN, WMAX +...  110 us

profile of v7, /device:TPU:7, one launch (start us, length us, event | category | flops | bytes accessed | tf_op | source)
XLA Modules:
  0.0 111.6 jit_solution(14774470875864864408)
XLA Ops:
  0.0 0.7 fusion
  0.7 109.7 %tiles.1 = f32[4,9,64,128]{3,2,1,0:T(8,128)S(1)} custom-call(bf16[64,32768]{1,0:T(8,128)(2,1)} %dos_ref.1), custom_call_target="tpu_custom_call" | custom-call | tf_op jit(solution)/shard_map/tiles/pallas_call | solution.py:335
  110.5 1.2 %multiply_select_fusion = f32[4,9,64,128]{3,2,1,0:T(8,128)} fusion(f32[4,9,64,128]{3,2,1,0:T(8,128)S(1)} %tiles.1, pred[4,9]{1,0:T(4,128)(4,1)S(1)} %fusion), kind=kLoop, calls=%fused_computation | loop fusion | flops 589824 | bytes 2359332 | tf_op jit(solution)/shard_map/jit(_where)/select_n | solution.py:382
  (1 shorter events, 0.0 us)

commit v8 on v6

--- a/solution.py
+++ b/solution.py
@@ -18,7 +18,7 @@
 LOCAL = GROUPS * ROWS
 BLOCK = 2 * PANEL
 STEPS = [(chunk, 0, CHUNK) for chunk in range(CHUNKS)]
-AHEAD = 24
+AHEAD = 30
 ORDER = [10, 15, 1, 4, 6, 3, 9, 12, 11, 14, 7, 13, 2, 8, 5]
 PARTNER = [1, 0, 3, 2, 5, 4, 7, 6, 9, 8, 11, 10, 13, 12, 14]
 SAMPLES = 8192

time: 111 us -> 111 us (level)
  no operation moved by 1% of the time
where the time goes in v8:
time: 111 us; the launch traced here: 110 us
  Pallas kernels  108 us (97%)
  other arithmetic  1.91 us (2%)
    pallas_call x1, Pallas kernels, tiles(): pl.pallas_call(tiles_kernel, out_shape=jax.ShapeDtypeStruct((OWN, WMAX +...  108 us

profile of v8, /device:TPU:7, one launch (start us, length us, event | category | flops | bytes accessed | tf_op | source)
XLA Modules:
  0.0 110.4 jit_solution(3069590827903332460)
XLA Ops:
  0.0 0.7 fusion
  0.7 108.5 %tiles.1 = f32[4,9,64,128]{3,2,1,0:T(8,128)S(1)} custom-call(bf16[64,32768]{1,0:T(8,128)(2,1)} %dos_ref.1), custom_call_target="tpu_custom_call" | custom-call | tf_op jit(solution)/shard_map/tiles/pallas_call | solution.py:335
  109.2 1.2 %multiply_select_fusion = f32[4,9,64,128]{3,2,1,0:T(8,128)} fusion(f32[4,9,64,128]{3,2,1,0:T(8,128)S(1)} %tiles.1, pred[4,9]{1,0:T(4,128)(4,1)S(1)} %fusion), kind=kLoop, calls=%fused_computation | loop fusion | flops 589824 | bytes 2359332 | tf_op jit(solution)/shard_map/jit(_where)/select_n | solution.py:382
  (1 shorter events, 0.0 us)
